TPU v7x, 32 devices: a whole 2x2x4 slice. The times are simulated.
32 devices in a mesh: grp: 4 (over y, x), fsdp: 4 (over z), ctx: 2 (over core).
Axes of the slice: x: 2, y: 2, z: 4, core: 2. Of those that a mesh axis runs over, the one named last changes fastest.
Arguments:
- activations_in: bfloat16 [2, 16, 1024, 1152], P(None, ('grp', 'fsdp'), 'ctx'), may hold values from -6 to 6
- prefix_len: int32 [2, 16], P(None, ('grp', 'fsdp')), may hold values from 102 to 512
- attn_gain: bfloat16 [1152], P(('fsdp', 'ctx')), may hold values from 0.5 to 1.5
- query_weight: bfloat16 [1152, 1152], P(('fsdp', 'ctx')), may hold values from -0.1875 to 0.1875
- key_weight: bfloat16 [1152, 384], P(('fsdp', 'ctx')), may hold values from -0.1875 to 0.1875
- value_weight: bfloat16 [1152, 384], P(('fsdp', 'ctx')), may hold values from -0.1875 to 0.1875
- out_weight: bfloat16 [1152, 1152], P(('fsdp', 'ctx')), may hold values from -0.75 to 0.75
- ffn_gain: bfloat16 [1152], P(('fsdp', 'ctx')), may hold values from 0.5 to 1.5
- gate_weight: bfloat16 [1152, 3072], P(('fsdp', 'ctx')), may hold values from -0.1875 to 0.1875
- up_weight: bfloat16 [1152, 3072], P(('fsdp', 'ctx')), may hold values from -0.1875 to 0.1875
- down_weight: bfloat16 [3072, 1152], P(('fsdp', 'ctx')), may hold values from -0.109375 to 0.109375
- cotangent: bfloat16 [2, 16, 1024, 1152], P(None, ('grp', 'fsdp'), 'ctx'), may hold values from -6 to 6
Outputs:
- activations_out: bfloat16 [2, 16, 1024, 1152], P(None, ('grp', 'fsdp'), 'ctx')
- input_grad: bfloat16 [2, 16, 1024, 1152], P(None, ('grp', 'fsdp'), 'ctx')
- grad_attn_gain: float32 [1152], P(('fsdp', 'ctx'))
- grad_query_weight: float32 [1152, 1152], P(('fsdp', 'ctx'))
- grad_key_weight: float32 [1152, 384], P(('fsdp', 'ctx'))
- grad_value_weight: float32 [1152, 384], P(('fsdp', 'ctx'))
- grad_out_weight: float32 [1152, 1152], P(('fsdp', 'ctx'))
- grad_ffn_gain: float32 [1152], P(('fsdp', 'ctx'))
- grad_gate_weight: float32 [1152, 3072], P(('fsdp', 'ctx'))
- grad_up_weight: float32 [1152, 3072], P(('fsdp', 'ctx'))
- grad_down_weight: float32 [3072, 1152], P(('fsdp', 'ctx'))
Inputs may be any that keep to these rules, and one draw needn't show every extreme that they name: prefix_len of a sequence is how many of its first positions every position of that sequence may attend to.
All inputs are finite; a program needn't handle non-finite values.
Results may differ from a plain program's by a relative error of at most 0.019.
Values may be sent and summed in bfloat16 or wider, within the bound.
A program may use at most 384 MiB of HBM per device.

v0:
```python
import math

import jax
import jax.numpy as jnp
from jax import lax
from jax.sharding import PartitionSpec as P

HEADS = 18
KV_HEADS = 6
HEAD = 64


epsilon = 1e-05


def shortened(array):

    def short(part):
        return part.astype(jnp.bfloat16) if part.dtype == jnp.float32 else part

    return jax.tree.map(short, array)


def rotary_tables(positions):
    halfway = HEAD // 2
    frequency = 10000.0 ** (-jnp.arange(halfway, dtype=jnp.float32) * 2.0 / HEAD)
    angles = positions.astype(jnp.float32)[:, None] * frequency[None, :]
    return (jnp.cos(angles)[:, None, :], jnp.sin(angles)[:, None, :])


def rotate(values, cosine, sine):
    halfway = values.shape[-1] // 2
    first = values[..., :halfway]
    second = values[..., halfway:]
    return jnp.concatenate([first * cosine - second * sine, second * cosine + first * sine], -1)


def rotate_back(values, cosine, sine):
    halfway = values.shape[-1] // 2
    first = values[..., :halfway]
    second = values[..., halfway:]
    return jnp.concatenate([first * cosine + second * sine, second * cosine - first * sine], -1)


def norm_back(grad_normed, normed, inverse):
    return inverse * (grad_normed - normed * jnp.mean(grad_normed * normed, -1, keepdims=True))


def flatten_all(grads):
    return tuple((g.reshape(-1) for g in grads))


def local(
    activations_in,
    prefix_len,
    attn_gain,
    query_weight,
    key_weight,
    value_weight,
    out_weight,
    ffn_gain,
    gate_weight,
    up_weight,
    down_weight,
    cotangent,
):
    micro, seq_count, span, width = activations_in.shape
    rows = seq_count * span
    length = span * lax.axis_size("ctx")
    groups = HEADS // KV_HEADS
    scale = 1.0 / math.sqrt(HEAD)
    shards = (
        attn_gain,
        query_weight,
        key_weight,
        value_weight,
        out_weight,
        ffn_gain,
        gate_weight,
        up_weight,
        down_weight,
    )
    offset = lax.axis_index("ctx") * span
    query_pos = offset + jnp.arange(span, dtype=jnp.int32)
    key_pos = jnp.arange(length, dtype=jnp.int32)
    cosine, sine = rotary_tables(jnp.tile(query_pos, seq_count))

    def visibility(prefix):
        return (key_pos[None, :] <= query_pos[:, None]) | (key_pos[None, :] < prefix)

    def attend(item):
        query, keys, values, prefix = item
        scores = (
            jnp.einsum("qhgd,khd->hgqk", query, keys, preferred_element_type=jnp.float32) * scale
        )
        scores = jnp.where(visibility(prefix), scores, -1e30)
        peak = jnp.max(scores, -1, keepdims=True)
        weights = jnp.exp(scores - peak)
        totals = jnp.sum(weights, -1, keepdims=True)
        probs = (weights / totals).astype(jnp.bfloat16)
        mixed = jnp.einsum("hgqk,khd->qhgd", probs, values, preferred_element_type=jnp.float32)
        return (mixed.reshape(span, HEADS * HEAD), (peak + jnp.log(totals))[..., 0])

    def attend_back(item):
        query, keys, values, prefix, log_total, grad_mixed = item
        scores = (
            jnp.einsum("qhgd,khd->hgqk", query, keys, preferred_element_type=jnp.float32) * scale
        )
        probs = jnp.where(visibility(prefix), jnp.exp(scores - log_total[..., None]), 0.0)
        grad_probs = jnp.einsum(
            "qhgd,khd->hgqk", grad_mixed, values, preferred_element_type=jnp.float32
        )
        grad_scores = (
            probs * (grad_probs - jnp.sum(probs * grad_probs, -1, keepdims=True))
        ).astype(jnp.bfloat16)
        grad_query = (
            jnp.einsum("hgqk,khd->qhgd", grad_scores, keys, preferred_element_type=jnp.float32)
            * scale
        )
        grad_keys = (
            jnp.einsum("hgqk,qhgd->khd", grad_scores, query, preferred_element_type=jnp.float32)
            * scale
        )
        grad_values = jnp.einsum(
            "hgqk,qhgd->khd",
            probs.astype(jnp.bfloat16),
            grad_mixed,
            preferred_element_type=jnp.float32,
        )
        return (
            grad_query.reshape(span, HEADS * HEAD),
            grad_keys.reshape(length, KV_HEADS * HEAD),
            grad_values.reshape(length, KV_HEADS * HEAD),
        )

    outputs = []
    input_grads = []
    collected = None
    for index in range(micro):
        full = (
            lax.all_gather(shards[0], ("fsdp", "ctx"), axis=0, tiled=True),
            lax.all_gather(shards[1], ("fsdp", "ctx"), axis=0, tiled=True),
            lax.all_gather(shards[2], ("fsdp", "ctx"), axis=0, tiled=True),
            lax.all_gather(shards[3], ("fsdp", "ctx"), axis=0, tiled=True),
            lax.all_gather(shards[4], ("fsdp", "ctx"), axis=0, tiled=True),
            lax.all_gather(shards[5], ("fsdp", "ctx"), axis=0, tiled=True),
            lax.all_gather(shards[6], ("fsdp", "ctx"), axis=0, tiled=True),
            lax.all_gather(shards[7], ("fsdp", "ctx"), axis=0, tiled=True),
            lax.all_gather(shards[8], ("fsdp", "ctx"), axis=0, tiled=True),
        )
        gain_attn, w_query, w_key, w_value, w_out, gain_ffn, w_gate, w_up, w_down = full
        inputs = activations_in[index].reshape(rows, width).astype(jnp.float32)
        inverse_one = lax.rsqrt(jnp.mean(inputs * inputs, -1, keepdims=True) + epsilon)
        normed_one = inputs * inverse_one
        first_in = (normed_one * gain_attn).astype(jnp.bfloat16)
        query_lin = jnp.dot(first_in, w_query, preferred_element_type=jnp.float32)
        key_lin = jnp.dot(first_in, w_key, preferred_element_type=jnp.float32)
        value_lin = jnp.dot(first_in, w_value, preferred_element_type=jnp.float32)
        query_rot = rotate(query_lin.reshape(rows, HEADS, HEAD), cosine, sine).astype(jnp.bfloat16)
        key_rot = rotate(key_lin.reshape(rows, KV_HEADS, HEAD), cosine, sine).astype(jnp.bfloat16)
        key_rot = key_rot.reshape(seq_count, span, KV_HEADS * HEAD)
        value_low = value_lin.astype(jnp.bfloat16).reshape(seq_count, span, KV_HEADS * HEAD)
        key_all, value_all = (
            lax.all_gather(key_rot, "ctx", axis=1, tiled=True),
            lax.all_gather(value_low, "ctx", axis=1, tiled=True),
        )
        query_split = query_rot.reshape(seq_count, span, KV_HEADS, groups, HEAD)
        key_split = key_all.reshape(seq_count, length, KV_HEADS, HEAD)
        value_split = value_all.reshape(seq_count, length, KV_HEADS, HEAD)
        mixed_all, log_totals = lax.map(
            attend, (query_split, key_split, value_split, prefix_len[index])
        )
        attn_low = mixed_all.reshape(rows, HEADS * HEAD).astype(jnp.bfloat16)
        middle = inputs + jnp.dot(attn_low, w_out, preferred_element_type=jnp.float32)
        inverse_two = lax.rsqrt(jnp.mean(middle * middle, -1, keepdims=True) + epsilon)
        normed_two = middle * inverse_two
        second_in = (normed_two * gain_ffn).astype(jnp.bfloat16)
        gate = jnp.dot(second_in, w_gate, preferred_element_type=jnp.float32)
        upward = jnp.dot(second_in, w_up, preferred_element_type=jnp.float32)
        hidden = (jax.nn.silu(gate) * upward).astype(jnp.bfloat16)
        result = middle + jnp.dot(hidden, w_down, preferred_element_type=jnp.float32)
        outputs.append(result.astype(jnp.bfloat16).reshape(seq_count, span, width))
        back = (
            lax.all_gather(shards[0], ("fsdp", "ctx"), axis=0, tiled=True),
            lax.all_gather(shards[1], ("fsdp", "ctx"), axis=0, tiled=True),
            lax.all_gather(shards[2], ("fsdp", "ctx"), axis=0, tiled=True),
            lax.all_gather(shards[3], ("fsdp", "ctx"), axis=0, tiled=True),
            lax.all_gather(shards[4], ("fsdp", "ctx"), axis=0, tiled=True),
            lax.all_gather(shards[5], ("fsdp", "ctx"), axis=0, tiled=True),
            lax.all_gather(shards[6], ("fsdp", "ctx"), axis=0, tiled=True),
            lax.all_gather(shards[7], ("fsdp", "ctx"), axis=0, tiled=True),
            lax.all_gather(shards[8], ("fsdp", "ctx"), axis=0, tiled=True),
        )
        gain_attn, w_query, w_key, w_value, w_out, gain_ffn, w_gate, w_up, w_down = back
        grad_y = cotangent[index].reshape(rows, width).astype(jnp.float32)
        grad_y_low = grad_y.astype(jnp.bfloat16)
        grad_wdown = jnp.einsum("rf,rd->fd", hidden, grad_y_low, preferred_element_type=jnp.float32)
        grad_hidden = jnp.einsum(
            "rd,fd->rf", grad_y_low, w_down, preferred_element_type=jnp.float32
        )
        sigma = jax.nn.sigmoid(gate)
        grad_up_low = (grad_hidden * gate * sigma).astype(jnp.bfloat16)
        grad_gate_low = (grad_hidden * upward * sigma * (1.0 + gate * (1.0 - sigma))).astype(
            jnp.bfloat16
        )
        grad_wgate = jnp.einsum(
            "rd,rf->df", second_in, grad_gate_low, preferred_element_type=jnp.float32
        )
        grad_wup = jnp.einsum(
            "rd,rf->df", second_in, grad_up_low, preferred_element_type=jnp.float32
        )
        grad_second = jnp.einsum(
            "rf,df->rd", grad_gate_low, w_gate, preferred_element_type=jnp.float32
        ) + jnp.einsum("rf,df->rd", grad_up_low, w_up, preferred_element_type=jnp.float32)
        grad_gain_ffn = jnp.sum(grad_second * normed_two, 0)
        grad_middle = grad_y + norm_back(grad_second * gain_ffn, normed_two, inverse_two)
        grad_branch_low = grad_middle.astype(jnp.bfloat16)
        grad_wout = jnp.einsum(
            "ra,rd->ad", attn_low, grad_branch_low, preferred_element_type=jnp.float32
        )
        grad_attn_low = jnp.einsum(
            "rd,ad->ra", grad_branch_low, w_out, preferred_element_type=jnp.float32
        ).astype(jnp.bfloat16)
        grad_mixed = grad_attn_low.reshape(seq_count, span, KV_HEADS, groups, HEAD)
        grad_query_rot, grad_key_part, grad_value_part = lax.map(
            attend_back,
            (query_split, key_split, value_split, prefix_len[index], log_totals, grad_mixed),
        )
        grad_key_own, grad_value_own = (
            lax.psum_scatter(
                grad_key_part.astype(jnp.bfloat16), "ctx", scatter_dimension=1, tiled=True
            ).astype(jnp.float32),
            lax.psum_scatter(
                grad_value_part.astype(jnp.bfloat16), "ctx", scatter_dimension=1, tiled=True
            ).astype(jnp.float32),
        )
        grad_query = rotate_back(grad_query_rot.reshape(rows, HEADS, HEAD), cosine, sine)
        grad_query = grad_query.reshape(rows, HEADS * HEAD).astype(jnp.bfloat16)
        grad_key = rotate_back(grad_key_own.reshape(rows, KV_HEADS, HEAD), cosine, sine)
        grad_key = grad_key.reshape(rows, KV_HEADS * HEAD).astype(jnp.bfloat16)
        grad_value = grad_value_own.reshape(rows, KV_HEADS * HEAD).astype(jnp.bfloat16)
        grad_wquery = jnp.einsum(
            "rd,rq->dq", first_in, grad_query, preferred_element_type=jnp.float32
        )
        grad_wkey = jnp.einsum("rd,rq->dq", first_in, grad_key, preferred_element_type=jnp.float32)
        grad_wvalue = jnp.einsum(
            "rd,rq->dq", first_in, grad_value, preferred_element_type=jnp.float32
        )
        grad_first = (
            jnp.einsum("rq,dq->rd", grad_query, w_query, preferred_element_type=jnp.float32)
            + jnp.einsum("rq,dq->rd", grad_key, w_key, preferred_element_type=jnp.float32)
            + jnp.einsum("rq,dq->rd", grad_value, w_value, preferred_element_type=jnp.float32)
        )
        grad_gain_attn = jnp.sum(grad_first * normed_one, 0)
        grad_inputs = grad_middle + norm_back(grad_first * gain_attn, normed_one, inverse_one)
        input_grads.append(grad_inputs.astype(jnp.bfloat16).reshape(seq_count, span, width))
        grads = flatten_all(
            (
                grad_gain_attn,
                grad_wquery,
                grad_wkey,
                grad_wvalue,
                grad_wout,
                grad_gain_ffn,
                grad_wgate,
                grad_wup,
                grad_wdown,
            )
        )
        pieces = lax.psum_scatter(grads, ("fsdp", "ctx"), scatter_dimension=0, tiled=True)
        if index == 0:
            collected = pieces
        else:
            collected = tuple((a + b for a, b in zip(collected, pieces)))
    summed = jax.tree.map(
        lambda part: part.astype(jnp.float32), lax.psum(shortened(collected), "grp")
    )
    shaped = tuple((s.reshape(w.shape) for s, w in zip(summed, shards)))
    return (
        jnp.stack(outputs, 0),
        jnp.stack(input_grads, 0),
        shaped[0],
        shaped[1],
        shaped[2],
        shaped[3],
        shaped[4],
        shaped[5],
        shaped[6],
        shaped[7],
        shaped[8],
    )


def solution(mesh):
    return jax.shard_map(
        local,
        mesh=mesh,
        in_specs=(
            P(None, ("grp", "fsdp"), "ctx", None),
            P(None, ("grp", "fsdp")),
            P(("fsdp", "ctx")),
            P(("fsdp", "ctx"), None),
            P(("fsdp", "ctx"), None),
            P(("fsdp", "ctx"), None),
            P(("fsdp", "ctx"), None),
            P(("fsdp", "ctx")),
            P(("fsdp", "ctx"), None),
            P(("fsdp", "ctx"), None),
            P(("fsdp", "ctx"), None),
            P(None, ("grp", "fsdp"), "ctx", None),
        ),
        out_specs=(
            P(None, ("grp", "fsdp"), "ctx", None),
            P(None, ("grp", "fsdp"), "ctx", None),
            P(("fsdp", "ctx")),
            P(("fsdp", "ctx"), None),
            P(("fsdp", "ctx"), None),
            P(("fsdp", "ctx"), None),
            P(("fsdp", "ctx"), None),
            P(("fsdp", "ctx")),
            P(("fsdp", "ctx"), None),
            P(("fsdp", "ctx"), None),
            P(("fsdp", "ctx"), None),
        ),
        check_vma=False,
    )
```

profile of v0, /device:TPU:0, one launch (start us, length us, event | category | flops | bytes accessed | tf_op | source)
XLA Modules:
  0.0 2008.6 jit_solution(11526617537344802159)
XLA Ops:
  10.7 21.4 %all_gather.27 = bf16[1152,384]{1,0:T(8,128)(2,1)} all-gather(bf16[144,384]{1,0:T(8,128)(2,1)S(1)} %copy-done.61), channel_id=1, replica_groups=mesh['grp'=4,'fsdp'=4,'ctx'=2] {'fsdp','ctx'}, dimensions={0}, use_global_device_ids=true | all-gather | bytes 995328 | tf_op jit(solution)/shard_map/all_gather | solution.py:144
  34.5 17.2 all-reduce.12
  51.7 18.8 all_gather.29
  115.8 15.2 fusion.10
  131.1 16.5 fusion.12
  147.6 18.1 fusion.65
  171.7 15.3 fusion.11
  187.0 16.6 fusion.13
  203.6 18.4 fusion.64
  238.7 9.9 fusion.145
  248.6 53.7 %all-gather.16.cloned.1.call-done = bf16[3072,1152]{1,0:T(8,128)(2,1)} async-done(((bf16[384,1152]{1,0:T(8,128)(2,1)}), bf16[3072,1152]{1,0:T(8,128)(2,1)}) %all-gather.16.cloned.1.call-update) | async-done | bytes 7077904 | tf_op jit(solution)/shard_map/all_gather | solution.py:149
  302.3 12.8 multiply_convert_fusion.2
  353.4 12.6 multiply_convert_fusion
  392.4 31.1 %fusion.3 = (f32[6,3,512]{2,1,0:T(4,128)S(1)}, f32[6,1024,512,3]{2,1,3,0:T(8,128)}) fusion(f32[6,1024,512,3]{2,1,3,0:T(8,128)} %get-tuple-element.215, f32[6,3,512]{2,1,0:T(4,128)S(1)} %copy-done.57, pred[512,1024]{0,1:T(8,128)(4,1)S(1)} %copy-done.1, bf16[1024,6,64,1]{0,2,3,1:T(8,128)(2,1)} %bitcast.404, bf16[512,6,3,64]{0,3,2,1:T(8,128)(2,1)} %bitcast.395), kind=kOutput, calls=%fused_computation.7 | convolution fusion | flops 1255136256 | bytes 78061568 | tf_op jit(solution)/shard_map/while/body/eval_jaxpr/qhgd,khd->hgqk/dot_general | solution.py:110
  423.5 31.3 %fusion.5 = bf16[6,3,512,1024]{2,3,1,0:T(8,128)(2,1)} fusion(f32[6,1024,512,3]{2,1,3,0:T(8,128)} %get-tuple-element.223, f32[6,1024,512,3]{2,1,3,0:T(8,128)} %get-tuple-element.215, f32[6,3,512]{2,1,0:T(4,128)S(1)} %get-tuple-element.222, f32[6,3,512]{2,1,0:T(4,128)S(1)} %copy-done.57, pred[512,1024]{0,1:T(8,128)(4,1)S(1)} %copy-done.1), kind=kLoop, calls=%fused_computation.9 | loop fusion | flops 56623104 | bytes 94969856 | tf_op jit(solution)/shard_map/while/body/eval_jaxpr/convert_element_type | solution.py:115
  454.8 11.5 convolution_multiply_fusion.1
  466.3 10.8 fusion.63
  500.2 30.2 %fusion = (f32[6,3,512]{2,1,0:T(4,128)S(1)}, f32[6,1024,512,3]{2,1,3,0:T(8,128)}) fusion(f32[6,1024,512,3]{2,1,3,0:T(8,128)} %get-tuple-element.213, f32[6,3,512]{2,1,0:T(4,128)S(1)} %copy-done.58, pred[512,1024]{0,1:T(8,128)(4,1)S(1)} %copy-done.4, bf16[1024,6,64,1]{0,2,3,1:T(8,128)(2,1)S(1)} %bitcast.402, bf16[512,6,3,64]{0,3,2,1:T(8,128)(2,1)S(1)} %bitcast.397), kind=kOutput, calls=%fused_computation.2 | convolution fusion | flops 1255136256 | bytes 78061568 | tf_op jit(solution)/shard_map/while/body/eval_jaxpr/qhgd,khd->hgqk/dot_general | solution.py:110
  530.3 31.5 %fusion.2 = bf16[6,3,512,1024]{2,3,1,0:T(8,128)(2,1)} fusion(f32[6,1024,512,3]{2,1,3,0:T(8,128)} %get-tuple-element.225, f32[6,1024,512,3]{2,1,3,0:T(8,128)} %get-tuple-element.213, f32[6,3,512]{2,1,0:T(4,128)S(1)} %get-tuple-element.224, f32[6,3,512]{2,1,0:T(4,128)S(1)} %copy-done.58, pred[512,1024]{0,1:T(8,128)(4,1)S(1)} %copy-done.4), kind=kLoop, calls=%fused_computation.4 | loop fusion | flops 56623104 | bytes 94969856 | tf_op jit(solution)/shard_map/while/body/eval_jaxpr/convert_element_type | solution.py:115
  561.9 11.5 convolution_multiply_fusion
  591.9 15.3 add_bitcast_fusion.1
  607.2 10.5 add_bitcast_fusion
  624.5 11.8 convolution_add_fusion
  649.8 13.4 copy.85
  663.3 13.4 copy.86
  676.7 15.3 reshape.652
  692.0 10.7 fusion.62
  702.8 17.4 bitcast_convert_fusion
  720.2 17.1 bitcast_convert_fusion.1
  768.1 13.7 reshape.647
  787.6 1090.4 %all-reduce.19 = (bf16[1152]{0:T(1024)(128)(2,1)S(1)}, bf16[1327104]{0:T(1024)(128)(2,1)}, bf16[442368]{0:T(1024)(128)(2,1)}, bf16[442368]{0:T(1024)(128)(2,1)},...) all-reduce(f32[1152]{0:T(1024)S(1)} %add.286, ...), channel_id=17, replica_groups=mesh['grp'=4,'fsdp'=4,'ctx'=2] {'fsdp','ctx'}, use_global_device_ids=true, to_apply=%region_19.20.clone | all-reduce | flops 14158080 | bytes 84948480
  1928.3 62.0 %all-reduce.18.cloned.1.call-done = (bf16[144,1152]{1,0:T(8,128)(2,1)}, bf16[144,384]{1,0:T(8,128)(2,1)}, bf16[144,384]{1,0:T(8,128)(2,1)}, bf16[144,1152]{1,0:T...) async-done(((bf16[144,1152]{1,0:T(8,128)(2,1)}, bf16[144,384]{1,0:T(8,128)(2,1)}, bf16[144,384]{1,0:T(8,128)(2,1)}, ...) | async-done | bytes 3538960 | tf_op jit(solution)/shard_map/psum | solution.py:276
  (311 shorter events, 294.3 us)
Async XLA Ops:
  7.2 24.9 %copy-start.5 = (bf16[2,1,512,1152]{3,2,1,0:T(8,128)(2,1)S(1)}, bf16[2,1,512,1152]{3,2,1,0:T(8,128)(2,1)}, u32[]{:S(2)}) copy-start(bf16[2,1,512,1152]{3,2,1,0:T(8,128)(2,1)} %param.12) | copy-start | bytes 7077892
  7.2 95.6 %all-gather.8.cloned.1.call-start = ((), (), s32[]{:S(2)}) async-start(), calls=%async_computation.4 | async-start | bytes 2985984 | tf_op jit(solution)/shard_map/all_gather | solution.py:142
  7.9 157.8 %all-gather.10.cloned.1.call-start = ((), (), s32[]{:S(2)}) async-start(), calls=%async_computation.5 | async-start | bytes 2985984 | tf_op jit(solution)/shard_map/all_gather | solution.py:145
  8.7 220.5 %all-gather.12.cloned.1.call-start = ((), (), s32[]{:S(2)}) async-start(), calls=%async_computation.6 | async-start | bytes 7962624 | tf_op jit(solution)/shard_map/all_gather | solution.py:147
  9.4 229.3 %all-gather.14.cloned.1.call-start = ((), (), s32[]{:S(2)}) async-start(), calls=%async_computation.7 | async-start | bytes 7962624 | tf_op jit(solution)/shard_map/all_gather | solution.py:148
  10.0 22.7 %copy-start.71 = (u32[32]{0:T(128)S(1)}, u32[32]{0:T(128)}, u32[]{:S(2)}) copy-start(u32[32]{0:T(128)} %constant.120) | copy-start | bytes 388
  10.0 23.9 %copy-start.74 = (bf16[144]{0:T(256)(128)(2,1)S(1)}, bf16[144]{0:T(256)(128)(2,1)}, u32[]{:S(2)}) copy-start(bf16[144]{0:T(256)(128)(2,1)} %param.14) | copy-start | bytes 868
  10.0 24.2 %copy-start.75 = (bf16[144]{0:T(256)(128)(2,1)S(1)}, bf16[144]{0:T(256)(128)(2,1)}, u32[]{:S(2)}) copy-start(bf16[144]{0:T(256)(128)(2,1)} %param.19) | copy-start | bytes 868
  10.0 41.7 %copy-start.62 = (bf16[144,384]{1,0:T(8,128)(2,1)S(1)}, bf16[144,384]{1,0:T(8,128)(2,1)}, u32[]{:S(2)}) copy-start(bf16[144,384]{1,0:T(8,128)(2,1)} %param.16) | copy-start | bytes 331780
  10.0 292.2 %all-gather.16.cloned.1.call-start = ((), (), s32[]{:S(2)}) async-start(), calls=%async_computation.8 | async-start | bytes 7962624 | tf_op jit(solution)/shard_map/all_gather | solution.py:149
  10.6 736.0 %reduce-scatter.5.cloned.1.call-start = ((), (), s32[]{:S(2)}) async-start(), calls=%async_computation.9 | async-start | bytes 1179648 | tf_op jit(solution)/shard_map/reduce_scatter | solution.py:230
  32.7 79.4 %copy-start.64 = (f32[512]{0:T(512)}, f32[512]{0:T(512)S(1)}, u32[]{:S(2)}) copy-start(f32[512]{0:T(512)S(1)} %add_rsqrt_fusion.1) | copy-start | bytes 6148
  51.7 60.4 %copy-start.59 = (f32[1152]{0:T(1024)}, f32[1152]{0:T(1024)S(1)}, u32[]{:S(2)}) copy-start(f32[1152]{0:T(1024)S(1)} %convert_element_type.375) | copy-start | bytes 13828
  72.0 36.3 %copy-start.67 = (f32[512]{0:T(512)}, f32[512]{0:T(512)S(1)}, u32[]{:S(2)}) copy-start(f32[512]{0:T(512)S(1)} %add_rsqrt_fusion.3) | copy-start | bytes 6148
  84.4 29.6 %copy-start.44 = (f32[512,32]{0,1:T(8,128)}, f32[512,32]{0,1:T(8,128)S(1)}, u32[]{:S(2)}) copy-start(f32[512,32]{0,1:T(8,128)S(1)} %get-tuple-element.204) | copy-start | bytes 196612
  84.4 29.6 %copy-start.46 = (f32[512,32]{0,1:T(8,128)}, f32[512,32]{0,1:T(8,128)S(1)}, u32[]{:S(2)}) copy-start(f32[512,32]{0,1:T(8,128)S(1)} %get-tuple-element.205) | copy-start | bytes 196612
  102.7 44.9 %copy-start = (pred[512,1024]{0,1:T(8,128)(4,1)}, pred[512,1024]{0,1:T(8,128)(4,1)S(1)}, u32[]{:S(2)}) copy-start(pred[512,1024]{0,1:T(8,128)(4,1)S(1)} %get-tuple-element.206) | copy-start | bytes 1572868
  102.7 100.9 %copy-start.3 = (pred[512,1024]{0,1:T(8,128)(4,1)}, pred[512,1024]{0,1:T(8,128)(4,1)S(1)}, u32[]{:S(2)}) copy-start(pred[512,1024]{0,1:T(8,128)(4,1)S(1)} %get-tuple-element.207) | copy-start | bytes 1572868
  115.8 15.3 copy-start.28
  115.8 15.3 copy-start.30
  238.7 63.6 %copy-start.24 = (bf16[2,1,512,1152]{3,2,1,0:T(8,128)(2,1)S(1)}, bf16[2,1,512,1152]{3,2,1,0:T(8,128)(2,1)}, u32[]{:S(2)}) copy-start(bf16[2,1,512,1152]{3,2,1,0:T(8,128)(2,1)} %param.23) | copy-start | bytes 7077892
  385.7 109.9 %copy-start.7 = (f32[512,1152]{1,0:T(8,128)}, f32[512,1152]{1,0:T(8,128)S(1)}, u32[]{:S(2)}) copy-start(f32[512,1152]{1,0:T(8,128)S(1)} %get-tuple-element.186) | copy-start | bytes 7077892
  500.1 30.2 %copy-start.33 = (bf16[512,1152]{0,1:T(8,128)(2,1)}, bf16[512,1152]{0,1:T(8,128)(2,1)S(1)}, u32[]{:S(2)}) copy-start(bf16[512,1152]{0,1:T(8,128)(2,1)S(1)} %copy.65) | copy-start | bytes 3538948
  573.4 174.3 %reduce-scatter.9.cloned.1.call-start = ((), (), s32[]{:S(2)}) async-start(), calls=%async_computation.11 | async-start | bytes 1179648 | tf_op jit(solution)/shard_map/reduce_scatter | solution.py:230
  591.9 15.3 copy-start.23
  591.9 15.3 copy-start.37
  617.7 18.6 slice-start
  702.7 17.5 copy-start.2
  702.7 53.3 %reduce-scatter.11.cloned.1.call-start = ((), (), s32[]{:S(2)}) async-start(), calls=%async_computation.12 | async-start | bytes 1179648 | tf_op jit(solution)/shard_map/reduce_scatter | solution.py:233
  720.1 40.2 %reduce-scatter.7.cloned.1.call-start = ((), (), s32[]{:S(2)}) async-start(), calls=%async_computation.10 | async-start | bytes 1179648 | tf_op jit(solution)/shard_map/reduce_scatter | solution.py:233
  737.3 1253.0 %all-reduce.18.cloned.1.call-start = ((), (), s32[]{:S(2)}) async-start(), calls=%async_computation.13 | async-start | bytes 7077888 | tf_op jit(solution)/shard_map/psum | solution.py:276
  768.1 13.7 copy-start.73
  (60 other events, 342.6 us)
Sparse Core Ops, SparseCore 0:
  9.7 40.4 all-gather.7
  51.8 34.9 all-gather.9
  88.4 71.0 all-gather.11
  161.0 69.8 all-gather.13
  232.4 69.8 all-gather.15
  573.6 6.8 reduce-scatter.4
  702.8 6.8 reduce-scatter.8
  720.3 6.8 reduce-scatter.10
  737.5 6.8 reduce-scatter.6
  1893.8 96.5 all-reduce.17
where the time goes:
time: 2010 us
  blocking collectives  1170 us (58%)
  matrix products  460 us (23%)
  other arithmetic  135 us (7%)
  waiting for transfers between devices  119 us (6%)
  local copies, waits for them, and re-layouts  107 us (5%)
    unnamed x2, blocking collectives  1110 us
    convert_element_type x2, other arithmetic, attend_back(): grad_scores = (probs * (grad_probs - jnp.sum(probs * grad_probs, -1, keep...  62.8 us
    psum x1, waiting for transfers between devices, local(): lax.psum(shortened(collected), 'grp')  62 us
    dot_general x2, matrix products, attend_back(): jnp.einsum('qhgd,khd->hgqk', grad_mixed, values, preferred_element_type=j...  61.2 us
    all_gather x1, waiting for transfers between devices, local(): lax.all_gather(shards[8], ('fsdp', 'ctx'), axis=0, tiled=True)  53.7 us
    add x5, local copies, waits for them, and re-layouts, local(): collected = tuple((a + b for a, b in zip(collected, pieces)))  44.9 us
    unnamed x180, local copies, waits for them, and re-layouts  40.3 us
  transfers between devices with their start and end apart: 10, of which 2 were waited for; matrix products, arithmetic and copies ran while one was open for 19% of the time, Pallas kernels for 0%

commit v1 on v0

--- a/solution.py
+++ b/solution.py
@@ -1,8 +1,12 @@
+import functools
 import math
 
 import jax
 import jax.numpy as jnp
+import numpy as np
 from jax import lax
+from jax.experimental import pallas as pl
+from jax.experimental.pallas import tpu as pltpu
 from jax.sharding import PartitionSpec as P
 
 HEADS = 18
@@ -291,9 +295,627 @@
     )
 
 
+GATHER_ORDER = ('f0', 's0', 'f1', 't0', 's1', 'f2', 't1', 's2', 'f3', 't2', 's3', 't3', 'l0', 'l1', 'l2', 'l3')
+MESH = pl.DeviceIdType.MESH
+
+def where_am_i():
+    return lax.axis_index("grp"), lax.axis_index("fsdp"), lax.axis_index("ctx")
+
+def remote(src, dst, send, recv, grp, fsdp, ctx):
+    return pltpu.make_async_remote_copy(src_ref=src, dst_ref=dst, send_sem=send, recv_sem=recv,
+        device_id={"grp": grp, "fsdp": fsdp, "ctx": ctx}, device_id_type=MESH)
+
+def greet(partners):
+    barrier = pltpu.get_barrier_semaphore()
+    for grp, fsdp, ctx in partners:
+        pl.semaphore_signal(barrier, inc=1, device_id={"grp": grp, "fsdp": fsdp, "ctx": ctx}, device_id_type=MESH)
+    pl.semaphore_wait(barrier, len(partners))
+
+
+class Column:
+    def __init__(self, shard, out):
+        self.shard, self.out = shard, out
+        self.rows = shard.shape[0]
+        self.block = out.shape[1] // 4
+    def mine(self, quarter, core):
+        return self.shard.at[:, pl.ds(pl.multiple_of((2 * quarter + core) * self.block, 128), self.block)]
+    def place(self, plane, core, quarter):
+        start = pl.multiple_of((2 * plane + core) * self.rows, 16)
+        return self.out.at[pl.ds(start, self.rows), pl.ds(pl.multiple_of(quarter * self.block, 128), self.block)]
+    def whole(self, plane, quarter):
+        start = pl.multiple_of(2 * plane * self.rows, 16)
+        return self.out.at[pl.ds(start, 2 * self.rows), pl.ds(pl.multiple_of(quarter * self.block, 128), self.block)]
+    def half(self, plane, quarter, which):
+        return self.place(plane, which, quarter)
+
+
+class Row:
+    def __init__(self, shard, out):
+        self.shard, self.out = shard, out
+        self.rows = shard.shape[0]
+        self.block = self.rows // 4
+    def mine(self, quarter):
+        return self.shard.at[pl.ds(pl.multiple_of(quarter * self.block, 16), self.block), :]
+    def whole(self, plane, quarter):
+        return self.out.at[pl.ds(pl.multiple_of(plane * self.rows + quarter * self.block, 16), self.block), :]
+    def half(self, plane, quarter, which):
+        size = self.block // 2
+        return self.out.at[pl.ds(pl.multiple_of(plane * self.rows + quarter * self.block + which * size, 16), size), :]
+
+
+def gather_kernel(order, *refs):
+    p_sh, g_sh, u_sh, d_sh, p_out, g_out, u_out, d_out, loc, near_s, near_r, z_s, z_r, xy_s, xy_r, fw_s, fw_r = refs
+    grp, plane, core = where_am_i()
+    side = grp + 1 - 2 * lax.rem(grp, 2)
+    up = lax.rem(grp + 2, 4)
+    planes = [lax.rem(plane + s, 4) for s in (1, 2, 3)]
+    origins = [lax.rem(plane + 4 - s, 4) for s in (1, 2, 3)]
+    partners = [(grp, z, c) for z in planes for c in (core, 1 - core)]
+    partners += [(grp, plane, 1 - core), (side, plane, core), (up, plane, core)]
+    greet(partners)
+    units = [Column(p_sh, p_out), Column(g_sh, g_out), Column(u_sh, u_out), Row(d_sh, d_out)]
+    tail = []
+
+    def first(n):
+        u = units[n]
+        if isinstance(u, Column):
+            for i, z in enumerate(planes):
+                for j, c in enumerate((core, 1 - core)):
+                    d = remote(u.mine(grp, c), u.place(plane, core, grp), z_s.at[n, i, j], z_r.at[n, i, j], grp, z, c)
+                    d.start(); tail.append(d.wait_send)
+            for q in range(4):
+                d = remote(u.mine(q, 1 - core), u.place(plane, core, q), near_s.at[n, q], near_r.at[n, q], grp, plane, 1 - core)
+                d.start(); tail.append(d.wait_send)
+                d = pltpu.make_async_copy(u.mine(q, core), u.place(plane, core, q), loc.at[n, q])
+                d.start(); tail.append(d.wait)
+        else:
+            for i, z in enumerate(planes):
+                d = remote(u.mine(grp), u.whole(plane, grp), z_s.at[n, i, 0], z_r.at[n, i, 0], grp, z, core)
+                d.start(); tail.append(d.wait_send)
+            d = pltpu.make_async_copy(u.shard, u.out.at[pl.ds(pl.multiple_of(plane * u.rows, 16), u.rows), :], loc.at[n, 0])
+            d.start(); tail.append(d.wait)
+
+    def second(n):
+        u = units[n]
+        for i, z in enumerate(origins):
+            if isinstance(u, Column):
+                for j, c in enumerate((core, 1 - core)):
+                    here = u.place(z, c, grp)
+                    remote(here, here, z_s.at[n, i, j], z_r.at[n, i, j], grp, z, c).wait_recv()
+            else:
+                here = u.whole(z, grp)
+                remote(here, here, z_s.at[n, i, 0], z_r.at[n, i, 0], grp, z, core).wait_recv()
+            here = u.whole(z, grp)
+            for j, to in enumerate((side, up)):
+                d = remote(here, here, xy_s.at[n, i, j], xy_r.at[n, i, j], to, plane, core)
+                d.start(); tail.append(d.wait_send)
+
+    def third(n):
+        u = units[n]
+        for i, z in enumerate(origins):
+            for j, (frm, to) in enumerate(((side, up), (up, side))):
+                here = u.whole(z, frm)
+                remote(here, here, xy_s.at[n, i, j], xy_r.at[n, i, j], frm, plane, core).wait_recv()
+                part = u.half(z, frm, j)
+                d = remote(part, part, fw_s.at[n, i, j], fw_r.at[n, i, j], to, plane, core)
+                d.start(); tail.append(d.wait_send)
+
+    def last(n):
+        u = units[n]
+        far = 3 - grp
+        for i, z in enumerate(origins):
+            for j, frm in enumerate((up, side)):
+                part = u.half(z, far, j)
+                remote(part, part, fw_s.at[n, i, j], fw_r.at[n, i, j], frm, plane, core).wait_recv()
+        if isinstance(u, Column):
+            for q in range(4):
+                here = u.place(plane, 1 - core, q)
+                remote(here, here, near_s.at[n, q], near_r.at[n, q], grp, plane, 1 - core).wait_recv()
+
+    ops = {'f': first, 's': second, 't': third, 'l': last}
+    for word in order: ops[word[0]](int(word[1]))
+    for w in tail: w()
+
+
+def gather(p, g, u, d):
+    out = lambda a, b: jax.ShapeDtypeStruct((a, b), jnp.bfloat16)
+    rows, cols = p.shape[0] * 8, p.shape[1] // 2
+    any_ = pl.BlockSpec(memory_space=pl.ANY)
+    dma = pltpu.SemaphoreType.DMA
+    return pl.pallas_call(functools.partial(gather_kernel, GATHER_ORDER),
+        out_shape=(out(rows, cols),) * 3 + (out(d.shape[0] * 4, d.shape[1]),),
+        in_specs=[any_] * 4, out_specs=(any_,) * 4,
+        scratch_shapes=[dma((4, 4)), dma((4, 4)), dma((4, 4)), dma((4, 3, 2)), dma((4, 3, 2)), dma((4, 3, 2)), dma((4, 3, 2)), dma((4, 3, 2)), dma((4, 3, 2))],
+        compiler_params=pltpu.CompilerParams(collective_id=0, has_side_effects=True),
+        name="gather_weights",
+    )(p, g, u, d)
+
+
+REDUCE_ORDER = ('a0', 'a1', 'b0', 'a2', 'b1', 'c0', 'a3', 'b2', 'c1', 'd0', 'b3', 'c2', 'd1', 'e0', 'c3', 'd2', 'e1', 'd3', 'e2', 'e3')
+
+def reduce_kernel(order, *refs):
+    grads, outs = refs[:4], refs[4:8]
+    accs, recvs, seconds, thirds, fins = refs[8:12], refs[12:16], refs[16:20], refs[20:24], refs[24:28]
+    load, s1, r1, s2, r2, s3, r3, s4, r4 = refs[28:]
+    grp, plane, core = where_am_i()
+    gx, gy = lax.rem(grp, 2), grp // 2
+    side, up = grp + 1 - 2 * gx, lax.rem(grp + 2, 4)
+    planes = [lax.rem(plane + s, 4) for s in (1, 2, 3)]
+    origins = [lax.rem(plane + 4 - s, 4) for s in (1, 2, 3)]
+    others = [lax.rem(grp + s, 4) for s in (1, 2, 3)]
+    sources = [lax.rem(grp + 4 - s, 4) for s in (1, 2, 3)]
+    partners = [(grp, z, core) for z in planes] + [(g, plane, c) for g in others for c in (core, 1 - core)] + [(grp, plane, 1 - core)]
+    greet(partners)
+    tail = []
+
+    def half(n, z, q, h):
+        ref = grads[n]
+        if n < 3:
+            rows, cols = ref.shape[0] // 8, ref.shape[1] // 4
+            return ref.at[pl.ds((2 * z + h) * rows, rows), pl.ds(pl.multiple_of(q * cols, 128), cols)]
+        rows = ref.shape[0] // 32
+        return ref.at[pl.ds(pl.multiple_of(((4 * z + q) * 2 + h) * rows, 16), rows), :]
+
+    def quarter(path, i, own):
+        if path == 0:
+            return 2 * i + (gx if own else 1 - gx)
+        return 2 * (gy if own else 1 - gy) + i
+
+    first_to, second_to = (side, up), (up, side)
+    keep = (gy, gx)
+
+    def a(n):
+        for z in range(4):
+            for path in range(2):
+                for i in range(2):
+                    d = pltpu.make_async_copy(half(n, z, quarter(path, i, True), path), accs[n].at[path, z, i], load.at[n, path, z, i])
+                    d.start()
+                    d = remote(half(n, z, quarter(path, i, False), path), recvs[n].at[path, z, i], s1.at[n, path, z, i], r1.at[n, path, z, i], first_to[path], plane, core)
+                    d.start(); tail.append(d.wait_send)
+
+    def b(n):
+        for z in range(4):
+            for path in range(2):
+                for i in range(2):
+                    here = accs[n].at[path, z, i]
+                    pltpu.make_async_copy(half(n, z, quarter(path, i, True), path), here, load.at[n, path, z, i]).wait()
+                    got = recvs[n].at[path, z, i]
+                    remote(got, got, s1.at[n, path, z, i], r1.at[n, path, z, i], first_to[path], plane, core).wait_recv()
+                    here[...] = (here[...].astype(jnp.float32) + got[...].astype(jnp.float32)).astype(jnp.bfloat16)
+                d = remote(accs[n].at[path, z, 1 - keep[path]], seconds[n].at[path, z], s2.at[n, path, z], r2.at[n, path, z], second_to[path], plane, core)
+                d.start(); tail.append(d.wait_send)
+
+    def c(n):
+        for z in range(4):
+            for path in range(2):
+                got = seconds[n].at[path, z]
+                remote(got, got, s2.at[n, path, z], r2.at[n, path, z], second_to[path], plane, core).wait_recv()
+                here = accs[n].at[path, z, keep[path]]
+                fins[n][z, path] = (here[...].astype(jnp.float32) + got[...].astype(jnp.float32)).astype(jnp.bfloat16)
+        for i, z in enumerate(planes):
+            d = remote(fins[n].at[z], thirds[n].at[i], s3.at[n, i], r3.at[n, i], grp, z, core)
+            d.start(); tail.append(d.wait_send)
+
+    def sent(n, which, to, c_to, i, j):
+        if n < 3:
+            rows, cols = outs[n].shape[0], outs[n].shape[1] // 8
+            dst = outs[n].at[:, pl.ds(pl.multiple_of((2 * which + c_to[1]) * cols, 128), cols)]
+            src = fins[n].at[plane, c_to[0]]
+            return src, dst
+        rows = outs[n].shape[0] // 8
+        dst = outs[n].at[pl.ds(pl.multiple_of((2 * which + j) * rows, 16), rows), :]
+        return fins[n].at[plane, j], dst
+
+    def d_(n):
+        for i, z in enumerate(origins):
+            got = thirds[n].at[i]
+            remote(got, got, s3.at[n, i], r3.at[n, i], grp, z, core).wait_recv()
+        for j in range(2):
+            total = fins[n][plane, j].astype(jnp.float32)
+            for i in range(3):
+                total += thirds[n][i, j].astype(jnp.float32)
+            fins[n][plane, j] = total.astype(jnp.bfloat16)
+        for j in range(2):
+            target = (core if j == 0 else 1 - core) if n < 3 else core
+            src, dst = sent(n, grp, None, (target, core), None, j)
+            if n < 3 and j == 1:
+                d = remote(src, dst, s4.at[n, 3, j], r4.at[n, 3, j], grp, plane, target)
+                d.start(); tail.append(d.wait_send)
+            else:
+                d = pltpu.make_async_copy(src, dst, s4.at[n, 3, j])
+                d.start(); tail.append(d.wait)
+            for i, g in enumerate(others):
+                d = remote(src, dst, s4.at[n, i, j], r4.at[n, i, j], g, plane, target)
+                d.start(); tail.append(d.wait_send)
+
+    def e(n):
+        for j in range(2):
+            origin = (core if j == 0 else 1 - core) if n < 3 else core
+            for i, g in enumerate(sources):
+                _, dst = sent(n, g, None, (core, origin), None, j)
+                remote(dst, dst, s4.at[n, i, j], r4.at[n, i, j], g, plane, origin).wait_recv()
+            if n < 3 and j == 1:
+                _, dst = sent(n, grp, None, (core, origin), None, j)
+                remote(dst, dst, s4.at[n, 3, j], r4.at[n, 3, j], grp, plane, origin).wait_recv()
+
+    ops = {"a": a, "b": b, "c": c, "d": d_, "e": e}
+    for word in order:
+        ops[word[0]](int(word[1]))
+    for w in tail:
+        w()
+
+
+def reduce_grads(*grads):
+    any_ = pl.BlockSpec(memory_space=pl.ANY)
+    dma = pltpu.SemaphoreType.DMA
+    halves = [(x.shape[0] // 8, x.shape[1] // 4) for x in grads[:3]] + [(grads[3].shape[0] // 32, grads[3].shape[1])]
+    def buf(*lead):
+        return [pltpu.VMEM(lead + h, jnp.bfloat16) for h in halves]
+    out = [jax.ShapeDtypeStruct((x.shape[0] // 8, x.shape[1] * 2), jnp.bfloat16) for x in grads[:3]] + [jax.ShapeDtypeStruct((grads[3].shape[0] // 4, grads[3].shape[1]), jnp.bfloat16)]
+    return pl.pallas_call(functools.partial(reduce_kernel, REDUCE_ORDER),
+        out_shape=tuple(out), in_specs=[any_] * 4, out_specs=(any_,) * 4,
+        scratch_shapes=buf(2, 4, 2) + buf(2, 4, 2) + buf(2, 4) + buf(3, 2) + buf(4, 2) + [
+            dma((4, 2, 4, 2)), dma((4, 2, 4, 2)), dma((4, 2, 4, 2)), dma((4, 2, 4)), dma((4, 2, 4)), dma((4, 3)), dma((4, 3)), dma((4, 4, 2)), dma((4, 4, 2))],
+        compiler_params=pltpu.CompilerParams(collective_id=1, has_side_effects=True, vmem_limit_bytes=48 * 2**20),
+        name="reduce_grads",
+    )(*grads)
+
+
+BLOCK = 256
+TO_LOG2 = math.log2(math.e) / math.sqrt(HEAD)
+F32, BF16 = jnp.float32, jnp.bfloat16
+NN = (((1,), (0,)), ((), ()))
+NT = (((1,), (1,)), ((), ()))
+TN = (((0,), (0,)), ((), ()))
+
+
+def dot(a, b, dims=NN):
+    return lax.dot_general(a, b, dims, preferred_element_type=F32)
+
+
+def turned(rows, cosine, sine, sign):
+    a, b = rows[: HEAD // 2], rows[HEAD // 2 :]
+    return jnp.concatenate([a * cosine - sign * b * sine, b * cosine + sign * a * sine], 0)
+
+
+def project_kernel(heads, kv_heads, x_ref, w_ref, cos_ref, sin_ref, n_ref, qt_ref, kvt_ref, kv_ref):
+    x = x_ref[...].astype(F32)
+    inverse = lax.rsqrt(jnp.mean(x * x, -1, keepdims=True) + epsilon)
+    normed = (x * inverse).astype(BF16)
+    n_ref[...] = normed
+    flat = dot(normed, w_ref[:, : (heads + 2 * kv_heads) * HEAD])
+    across = flat.T
+    cosine, sine = cos_ref[...], sin_ref[...]
+    for h in range(heads):
+        rows = turned(across[h * HEAD : (h + 1) * HEAD], cosine, sine, 1.0)
+        qt_ref[h * HEAD : (h + 1) * HEAD, :] = (rows * TO_LOG2).astype(BF16)
+    base = heads * HEAD
+    keys = jnp.concatenate([turned(across[base + h * HEAD : base + (h + 1) * HEAD], cosine, sine, 1.0) for h in range(kv_heads)], 0)
+    kv_width = kv_heads * HEAD
+    values = across[base + kv_width : base + 2 * kv_width]
+    kvt_ref[:kv_width, :] = keys.astype(BF16)
+    kvt_ref[kv_width:, :] = values.astype(BF16)
+    kv_ref[:, :kv_width] = keys.T.astype(BF16)
+    kv_ref[:, kv_width:] = flat[:, base + kv_width : base + 2 * kv_width].astype(BF16)
+
+
+def project(x, weight, cosine, sine, heads, kv_heads, length):
+    tokens, width = x.shape
+    cols = (heads + 2 * kv_heads) * HEAD
+    per = length // BLOCK
+    return pl.pallas_call(
+        functools.partial(project_kernel, heads, kv_heads),
+        grid=(tokens // BLOCK,),
+        in_specs=[
+            pl.BlockSpec((BLOCK, width), lambda i: (i, 0)),
+            pl.BlockSpec((width, -(-cols // 128) * 128), lambda i: (0, 0)),
+            pl.BlockSpec((HEAD // 2, BLOCK), lambda i: (0, lax.rem(i, per))),
+            pl.BlockSpec((HEAD // 2, BLOCK), lambda i: (0, lax.rem(i, per))),
+        ],
+        out_specs=(
+            pl.BlockSpec((BLOCK, width), lambda i: (i, 0)),
+            pl.BlockSpec((heads * HEAD, BLOCK), lambda i: (0, i)),
+            pl.BlockSpec((2 * kv_heads * HEAD, BLOCK), lambda i: (0, i)),
+            pl.BlockSpec((BLOCK, 2 * kv_heads * HEAD), lambda i: (i, 0)),
+        ),
+        out_shape=(
+            jax.ShapeDtypeStruct((tokens, width), BF16),
+            jax.ShapeDtypeStruct((heads * HEAD, tokens), BF16),
+            jax.ShapeDtypeStruct((2 * kv_heads * HEAD, tokens), BF16),
+            jax.ShapeDtypeStruct((tokens, 2 * kv_heads * HEAD), BF16),
+        ),
+        compiler_params=pltpu.CompilerParams(vmem_limit_bytes=48 * 2**20),
+        cost_estimate=pl.CostEstimate(flops=2 * tokens * width * cols, bytes_accessed=4 * tokens * (width + cols), transcendentals=0),
+        name="project",
+    )(x, weight, cosine, sine)
+
+
+def masked(scores, prefix, first, block):
+    key = first + lax.broadcasted_iota(jnp.int32, scores.shape, 0)
+    query = block * BLOCK + lax.broadcasted_iota(jnp.int32, scores.shape, 1)
+    return jnp.where((key <= query) | (key < prefix), scores, -1e30)
+
+
+def reach(block):
+    return max(2, block + 1) * BLOCK
+
+
+def scores_of(keys, query, prefix, block):
+    clear = block * BLOCK
+    edge = masked(dot(keys[clear:], query), prefix, clear, block)
+    if not clear:
+        return edge
+    return jnp.concatenate([dot(keys[:clear], query), edge], 0)
+
+
+def attend_kernel(heads, kv_heads, blocks, prefix_ref, qt_ref, kv_ref, vt_ref, wo_ref, ot_ref, lse_ref, part_ref):
+    prefix = prefix_ref[pl.program_id(0)]
+    groups = heads // kv_heads
+
+    def run(block):
+        n = reach(block)
+        for kh in range(kv_heads):
+            keys = kv_ref[:n, kh * HEAD : (kh + 1) * HEAD]
+            vt = vt_ref[kh * HEAD : (kh + 1) * HEAD, :n]
+            for h in range(kh * groups, (kh + 1) * groups):
+                scores = scores_of(keys, qt_ref[h * HEAD : (h + 1) * HEAD, :], prefix, block)
+                peak = jnp.max(scores, 0, keepdims=True)
+                weights = jnp.exp2(scores - peak)
+                total = jnp.sum(weights, 0, keepdims=True)
+                mixed = dot(vt, weights.astype(BF16)) / total
+                ot_ref[h * HEAD : (h + 1) * HEAD, :] = mixed.astype(BF16)
+                lse_ref[h : h + 1, :] = peak + jnp.log2(total)
+
+    for block in range(blocks):
+        pl.when(pl.program_id(1) == block)(functools.partial(run, block))
+    part_ref[...] = dot(ot_ref[...], wo_ref[...], TN).astype(BF16)
+
+
+def attend(prefix, qt, kv, kvt, wo, heads, kv_heads, length):
+    tokens = qt.shape[1]
+    width = wo.shape[1]
+    count, blocks = tokens // length, length // BLOCK
+    kv_width = kv_heads * HEAD
+    cells = count * heads * sum(reach(b) for b in range(blocks)) * BLOCK
+    return pl.pallas_call(
+        functools.partial(attend_kernel, heads, kv_heads, blocks),
+        grid=(count, blocks),
+        in_specs=[
+            pl.BlockSpec(memory_space=pltpu.SMEM),
+            pl.BlockSpec((heads * HEAD, BLOCK), lambda s, i: (0, s * blocks + i)),
+            pl.BlockSpec((length, 2 * kv_width), lambda s, i: (s, 0)),
+            pl.BlockSpec((kv_width, length), lambda s, i: (1, s)),
+            pl.BlockSpec((heads * HEAD, width), lambda s, i: (0, 0)),
+        ],
+        out_specs=(
+            pl.BlockSpec((heads * HEAD, BLOCK), lambda s, i: (0, s * blocks + i)),
+            pl.BlockSpec((heads, BLOCK), lambda s, i: (0, s * blocks + i)),
+            pl.BlockSpec((BLOCK, width), lambda s, i: (s * blocks + i, 0)),
+        ),
+        out_shape=(
+            jax.ShapeDtypeStruct((heads * HEAD, tokens), BF16),
+            jax.ShapeDtypeStruct((heads, tokens), F32),
+            jax.ShapeDtypeStruct((tokens, width), BF16),
+        ),
+        compiler_params=pltpu.CompilerParams(vmem_limit_bytes=48 * 2**20),
+        cost_estimate=pl.CostEstimate(flops=4 * cells * 256, bytes_accessed=8 * tokens * width, transcendentals=cells),
+        name="attend",
+    )(prefix, qt, kv, kvt, wo)
+
+
+def attend_back_kernel(heads, kv_heads, blocks, prefix_ref, qt_ref, kv_ref, kt_ref, ot_ref, lse_ref, dx_ref, wo_ref,
+                       cos_ref, sin_ref, cos_all, sin_all, dqt_ref, dkvt_ref, dot_ref, dk_ref, dv_ref):
+    prefix = prefix_ref[pl.program_id(0)]
+    groups = heads // kv_heads
+    kv_width = kv_heads * HEAD
+    at = pl.program_id(1)
+    dot_ref[...] = dot(wo_ref[...], dx_ref[...], NT).astype(BF16)
+
+    @pl.when(at == 0)
+    def _():
+        dk_ref[...] = jnp.zeros_like(dk_ref)
+        dv_ref[...] = jnp.zeros_like(dv_ref)
+
+    def run(block):
+        n = reach(block)
+        for kh in range(kv_heads):
+            keys = kv_ref[:n, kh * HEAD : (kh + 1) * HEAD]
+            values = kv_ref[:n, kv_width + kh * HEAD : kv_width + (kh + 1) * HEAD]
+            kt = kt_ref[kh * HEAD : (kh + 1) * HEAD, :n]
+            for h in range(kh * groups, (kh + 1) * groups):
+                own = slice(h * HEAD, (h + 1) * HEAD)
+                query, grad = qt_ref[own, :], dot_ref[own, :]
+                delta = jnp.sum(grad.astype(F32) * ot_ref[own, :].astype(F32), 0, keepdims=True)
+                scores = scores_of(keys, query, prefix, block)
+                probs = jnp.exp2(scores - lse_ref[h : h + 1, :])
+                grad_probs = dot(values, grad)
+                grad_scores = (probs * (grad_probs - delta)).astype(BF16)
+                dv_ref[kh, :n, :] += dot(probs.astype(BF16), grad, NT)
+                dk_ref[kh, :n, :] += dot(grad_scores, query, NT)
+                grad_query = dot(kt, grad_scores)
+                dqt_ref[own, :] = (turned(grad_query, cos_ref[...], sin_ref[...], -1.0) * (1.0 / math.sqrt(HEAD))).astype(BF16)
+
+    for block in range(blocks):
+        pl.when(at == block)(functools.partial(run, block))
+
+    @pl.when(at == blocks - 1)
+    def _():
+        for kh in range(kv_heads):
+            rows = turned(dk_ref[kh].T, cos_all[...], sin_all[...], -1.0) * math.log(2.0)
+            dkvt_ref[kh * HEAD : (kh + 1) * HEAD, :] = rows.astype(BF16)
+            dkvt_ref[kv_width + kh * HEAD : kv_width + (kh + 1) * HEAD, :] = dv_ref[kh].T.astype(BF16)
+
+
+def attend_back(prefix, qt, kv, kvt, ot, lse, dx, wo, cosine, sine, heads, kv_heads, length):
+    tokens = qt.shape[1]
+    width = wo.shape[1]
+    count, blocks = tokens // length, length // BLOCK
+    kv_width = kv_heads * HEAD
+    cells = count * heads * sum(reach(b) for b in range(blocks)) * BLOCK
+    tile = pl.BlockSpec((heads * HEAD, BLOCK), lambda s, i: (0, s * blocks + i))
+    table = pl.BlockSpec((HEAD // 2, BLOCK), lambda s, i: (0, i))
+    whole = pl.BlockSpec((HEAD // 2, length), lambda s, i: (0, 0))
+    return pl.pallas_call(
+        functools.partial(attend_back_kernel, heads, kv_heads, blocks),
+        grid=(count, blocks),
+        in_specs=[
+            pl.BlockSpec(memory_space=pltpu.SMEM),
+            tile,
+            pl.BlockSpec((length, 2 * kv_width), lambda s, i: (s, 0)),
+            pl.BlockSpec((kv_width, length), lambda s, i: (0, s)),
+            tile,
+            pl.BlockSpec((heads, BLOCK), lambda s, i: (0, s * blocks + i)),
+            pl.BlockSpec((BLOCK, width), lambda s, i: (s * blocks + i, 0)),
+            pl.BlockSpec((heads * HEAD, width), lambda s, i: (0, 0)),
+            table, table, whole, whole,
+        ],
+        out_specs=(tile, pl.BlockSpec((2 * kv_width, length), lambda s, i: (0, s))),
+        out_shape=(
+            jax.ShapeDtypeStruct((heads * HEAD, tokens), BF16),
+            jax.ShapeDtypeStruct((2 * kv_width, tokens), BF16),
+        ),
+        scratch_shapes=[
+            pltpu.VMEM((heads * HEAD, BLOCK), BF16),
+            pltpu.VMEM((kv_heads, length, HEAD), F32),
+            pltpu.VMEM((kv_heads, length, HEAD), F32),
+        ],
+        compiler_params=pltpu.CompilerParams(vmem_limit_bytes=48 * 2**20),
+        cost_estimate=pl.CostEstimate(flops=10 * cells * 256, bytes_accessed=12 * tokens * width, transcendentals=cells),
+        name="attend_back",
+    )(prefix, qt, kv, kvt, ot, lse, dx, wo, cosine, sine, cosine, sine)
+
+
+SWAP = [(0, 1), (1, 0)]
+
+
+def trade(mine):
+    return lax.ppermute(mine, "ctx", SWAP)
+
+
+def ordered(core, mine, other, axis):
+    return jnp.concatenate([jnp.where(core == 0, mine, other), jnp.where(core == 0, other, mine)], axis)
+
+
+def part_of(array, which, axis):
+    size = array.shape[axis] // 2
+    return lax.dynamic_slice_in_dim(array, which * size, size, axis)
+
+
+def tables(length):
+    frequency = np.float32(10000.0) ** (-np.arange(HEAD // 2, dtype=np.float32) * np.float32(2.0) / np.float32(HEAD))
+    angles = frequency[:, None] * np.arange(length, dtype=np.float32)[None, :]
+    return jnp.asarray(np.cos(angles)), jnp.asarray(np.sin(angles))
+
+
+def paired(
+    activations_in,
+    prefix_len,
+    attn_gain,
+    query_weight,
+    key_weight,
+    value_weight,
+    out_weight,
+    ffn_gain,
+    gate_weight,
+    up_weight,
+    down_weight,
+    cotangent,
+):
+    micro, seq_count, span, width = activations_in.shape
+    count, length = micro * seq_count, 2 * span
+    core = lax.axis_index("ctx")
+    heads, kv_heads = HEADS // 2, KV_HEADS // 2
+    q_cols, kv_cols = heads * HEAD, kv_heads * HEAD
+    shard = attn_gain.shape[0]
+
+    own_x = activations_in.reshape(count, span, width)
+    own_dy = cotangent.reshape(count, span, width)
+
+    def whole(mine):
+        return ordered(core, mine, trade(mine), 1).reshape(count * length, width)
+
+    def summed(part):
+        part = part.reshape(count, length, width)
+        theirs = trade(part_of(part, 1 - core, 1))
+        return part_of(part, core, 1).astype(F32) + theirs.astype(F32)
+
+    gain_attn = attn_gain.astype(F32)[:, None]
+    gain_ffn = ffn_gain.astype(F32)[:, None]
+    qkv = [w.astype(F32) for w in (query_weight, key_weight, value_weight)]
+    first = [(w * gain_attn).astype(BF16).reshape(shard, 2, -1) for w in qkv]
+    pack = jnp.concatenate(first + [out_weight.reshape(shard, 2, -1)], -1)
+    pack = pack.reshape(shard, 2, 4, -1).swapaxes(1, 2).reshape(shard, -1)
+    w_pack, w_gate, w_up, w_down = gather(
+        pack, (gate_weight * gain_ffn).astype(BF16), (up_weight * gain_ffn).astype(BF16), down_weight
+    )
+    w_out_cols = w_pack[:, q_cols + 2 * kv_cols :]
+    w_out = ordered(core, part_of(w_out_cols, core, 0), trade(part_of(w_out_cols, 1 - core, 0)), 1)
+
+    cosine, sine = tables(length)
+    prefix = prefix_len.reshape(count)
+    full_x, full_dy = whole(own_x), whole(own_dy)
+    normed_one, qt, kvt, kv = project(full_x, w_pack, cosine, sine, heads, kv_heads, length)
+    ot, lse, part = attend(prefix, qt, kv, kvt, w_out, heads, kv_heads, length)
+    middle = own_x.astype(F32) + summed(part)
+    inverse_two = lax.rsqrt(jnp.mean(middle * middle, -1, keepdims=True) + epsilon)
+    normed_two = middle * inverse_two
+    full_two = whole(normed_two.astype(BF16))
+    gate = dot(full_two, w_gate)
+    upward = dot(full_two, w_up)
+    hidden = (jax.nn.silu(gate) * upward).astype(BF16)
+    result = middle + summed(dot(hidden, w_down).astype(BF16))
+
+    gate, upward = gate.astype(BF16).astype(F32), upward.astype(BF16).astype(F32)
+    grad_down = dot(hidden, full_dy, TN).astype(BF16)
+    grad_hidden = dot(full_dy, w_down, NT)
+    sigma = jax.nn.sigmoid(gate)
+    d_up = (grad_hidden * gate * sigma).astype(BF16)
+    d_gate = (grad_hidden * upward * sigma * (1.0 + gate * (1.0 - sigma))).astype(BF16)
+    grad_gate = dot(full_two, d_gate, TN).astype(BF16)
+    grad_up = dot(full_two, d_up, TN).astype(BF16)
+    grad_two = summed((dot(d_gate, w_gate, NT) + dot(d_up, w_up, NT)).astype(BF16))
+    grad_middle = own_dy.astype(F32) + norm_back(grad_two, normed_two, inverse_two)
+    full_dx = whole(grad_middle.astype(BF16))
+    grad_out_rows = dot(ot, full_dx).astype(BF16)
+    dqt, dkvt = attend_back(prefix, qt, kv, kvt, ot, lse, full_dx, w_out, cosine, sine, heads, kv_heads, length)
+    dt = jnp.concatenate([dqt, dkvt], 0)
+    grad_qkv = dot(normed_one, dt, (((0,), (1,)), ((), ()))).astype(BF16)
+    grad_one = summed(dot(dt, w_pack[:, : q_cols + 2 * kv_cols], (((0,), (1,)), ((), ()))).astype(BF16))
+    x = own_x.astype(F32)
+    inverse_one = lax.rsqrt(jnp.mean(x * x, -1, keepdims=True) + epsilon)
+    grad_inputs = grad_middle + norm_back(grad_one, x * inverse_one, inverse_one)
+
+    grad_out_cols = ordered(core, part_of(grad_out_rows, core, 1), trade(part_of(grad_out_rows, 1 - core, 1)), 0)
+    grad_pack = jnp.concatenate([grad_qkv, grad_out_cols], 1)
+    r_pack, r_gate, r_up, r_down = (g.astype(F32) for g in reduce_grads(grad_pack, grad_gate, grad_up, grad_down))
+    r_pack = r_pack.reshape(shard, 4, 2, -1).swapaxes(1, 2).reshape(shard, 2, -1)
+    r_q, r_k, r_v, r_out = (
+        piece.reshape(shard, -1)
+        for piece in jnp.split(r_pack, [q_cols, q_cols + kv_cols, q_cols + 2 * kv_cols], axis=2)
+    )
+    grad_gain_attn = sum(jnp.sum(w * r, -1) for w, r in zip(qkv, (r_q, r_k, r_v)))
+    grad_gain_ffn = jnp.sum(gate_weight * r_gate, -1) + jnp.sum(up_weight * r_up, -1)
+    shape = activations_in.shape
+    return (
+        result.astype(BF16).reshape(shape),
+        grad_inputs.astype(BF16).reshape(shape),
+        grad_gain_attn,
+        r_q * gain_attn,
+        r_k * gain_attn,
+        r_v * gain_attn,
+        r_out,
+        grad_gain_ffn,
+        r_gate * gain_ffn,
+        r_up * gain_ffn,
+        r_down,
+    )
+
+
 def solution(mesh):
+    small = dict(mesh.shape) == {"grp": 4, "fsdp": 4, "ctx": 2}
+
     return jax.shard_map(
-        local,
+        paired if small else local,
         mesh=mesh,
         in_specs=(
             P(None, ("grp", "fsdp"), "ctx", None),

time: 2010 us -> 641 us (0.32)
  blocking collectives: 1170 us -> 0 us
  Pallas kernels: 0 us -> 367 us
  matrix products: 460 us -> 137 us
  waiting for transfers between devices: 119 us -> 10.1 us
  other arithmetic: 135 us -> 57.7 us
  local copies, waits for them, and re-layouts: 107 us -> 57.3 us
    unnamed x2 -> x0, blocking collectives: 1110 us -> none
    pallas_call x0 -> x5, Pallas kernels: none -> 367 us  [the longest x1 165 us: reduce_grads(): pl.pallas_call(functools.partial(reduce_kernel, REDUCE_ORDER), out_shape=...]
    dot_general x54 -> x12, matrix products: 460 us -> 137 us  [dot(): return lax.dot_general(a, b, dims, preferred_element_type=F32)]
    psum x1 -> x0, waiting for transfers between devices: 62 us -> none  [local(): lax.psum(shortened(collected), 'grp')]
    convert_element_type x11 -> x8, other arithmetic: 65 us -> 11.3 us  [the longest x1 4.45 us: paired(): full_dx = whole(grad_middle.astype(BF16))]
    all_gather x5 -> x0, waiting for transfers between devices: 53.7 us -> none  [the longest x1 53.7 us: local(): lax.all_gather(shards[8], ('fsdp', 'ctx'), axis=0, tiled=True)]
    all_gather x6 -> x0, blocking collectives: 50.6 us -> none  [the longest x1 21.4 us: local(): lax.all_gather(shards[3], ('fsdp', 'ctx'), axis=0, tiled=True)]
    add x5 -> x0, local copies, waits for them, and re-layouts: 44.9 us -> none  [local(): collected = tuple((a + b for a, b in zip(collected, pieces)))]
  transfers between devices with their start and end apart: 10 -> 10, of which waited for: 2 -> 3; matrix products, arithmetic and copies ran while one was open for 19% -> 20% of each run, Pallas kernels for 0% -> 49%
where the time goes in v1:
time: 641 us; the launch traced here: 634 us
  Pallas kernels  367 us (57%)
  matrix products  137 us (21%)
  other arithmetic  57.7 us (9%)
  local copies, waits for them, and re-layouts  57.3 us (9%)
  waiting for transfers between devices  10.1 us (2%)
    pallas_call x1, Pallas kernels, reduce_grads(): pl.pallas_call(functools.partial(reduce_kernel, REDUCE_ORDER), out_shape=...  165 us
    dot_general x12, matrix products, dot(): return lax.dot_general(a, b, dims, preferred_element_type=F32)  137 us
    pallas_call x1, Pallas kernels, gather(): pl.pallas_call(functools.partial(gather_kernel, GATHER_ORDER), out_shape=...  106 us
    pallas_call x1, Pallas kernels, attend_back(): pl.pallas_call(functools.partial(attend_back_kernel, heads, kv_heads, blo...  42.6 us
    pallas_call x1, Pallas kernels, attend(): pl.pallas_call(functools.partial(attend_kernel, heads, kv_heads, blocks),...  40.9 us
    unnamed x115, local copies, waits for them, and re-layouts  13.2 us
    pallas_call x1, Pallas kernels, project(): pl.pallas_call(functools.partial(project_kernel, heads, kv_heads), grid=(...  12.8 us
  transfers between devices with their start and end apart: 10, of which 3 were waited for; matrix products, arithmetic and copies ran while one was open for 20% of the time, Pallas kernels for 49%

profile of v1, /device:TPU:0, one launch (start us, length us, event | category | flops | bytes accessed | tf_op | source)
XLA Modules:
  0.0 633.6 jit_solution(14770356302111493415)
XLA Ops:
  7.3 4.6 concatenate.28
  15.3 106.2 %gather_weights.1 = (bf16[1152,1536]{1,0:T(8,128)(2,1)}, bf16[1152,1536]{1,0:T(8,128)(2,1)}, bf16[1152,1536]{1,0:T(8,128)(2,1)}, bf16[1536,1152]{1,0:T(8,128)(2,1)}) custom-call(bf16[144,3072]{1,0:T(8,128)(2,1)} %reshape.135.refs_0_, bf16[144,3072]{1,0:T(8,128)(2,1)} %get-tuple-element.84.refs_1_, bf16[144,3072]{1,0:T(8,128)(2,1)} %get-tuple-element.83.refs_2_, ...), custom_call_target="tpu_custom_call" | custom-call | tf_op jit(solution)/shard_map/gather_weights/pallas_call | solution.py:425
  121.4 3.3 slice.6
  136.2 12.8 %project.1 = (bf16[2048,1152]{1,0:T(8,128)(2,1)}, bf16[576,2048]{1,0:T(8,128)(2,1)S(1)}, bf16[384,2048]{1,0:T(8,128)(2,1)S(1)}, bf16[2048,384]{1,0:T(8,128)(2,1)S(1)}) custom-call(bf16[2048,1152]{1,0:T(8,128)(2,1)} %bitcast.88, bf16[1152,1536]{1,0:T(8,128)(2,1)} %get-tuple-element.28.w_ref, f32[32,1024]{1,0:T(8,128)S(1)} %copy-done.6, f32[32,1024]{1,0:T(8,128)S(1)} %copy-done.4), custom_call_target="tpu_custom_call" | custom-call | flops 4529848320 | bytes 17301504 | tf_op jit(solution)/shard_map/project/pallas_call | solution.py:606
  150.5 40.9 %attend.1 = (bf16[576,2048]{1,0:T(8,128)(2,1)}, f32[9,2048]{1,0:T(8,128)S(1)}, bf16[2048,1152]{1,0:T(8,128)(2,1)}) custom-call(s32[2]{0:T(128)S(1)} %bitcast.58, bf16[576,2048]{1,0:T(8,128)(2,1)} %copy-done.8, bf16[2048,384]{1,0:T(8,128)(2,1)S(1)} %get-tuple-element.30.kv_ref, bf16[384,2048]{1,0:T(8,128)(2,1)S(1)} %get-tuple-element.31.vt_ref.kt_ref, ...), custom_call_target="tpu_custom_call" | custom-call | flops 13287555072 | bytes 18874368 | tf_op jit(solution)/shard_map/attend/pallas_call | solution.py:680
  191.4 3.3 constant_dynamic-slice_fusion.4
  195.2 4.4 collective-permute-done.2
  199.5 3.9 multiply_reduce_fusion.1
  205.0 3.4 collective-permute-done.3
  211.8 3.3 copy-done.43
  215.1 10.9 %fusion.33 = f32[2048,1536]{1,0:T(8,128)} fusion(bf16[2048,1152]{1,0:T(8,128)(2,1)S(1)} %bitcast.78, bf16[1152,1536]{1,0:T(8,128)(2,1)S(1)} %copy-done.43), kind=kOutput, calls=%fused_computation.101 | convolution fusion | flops 7247757312 | bytes 20840448 | tf_op jit(solution)/shard_map/dot_general | solution.py:573
  226.0 10.8 %fusion.32 = f32[2048,1536]{1,0:T(8,128)} fusion(bf16[2048,1152]{1,0:T(8,128)(2,1)S(1)} %bitcast.79, bf16[1152,1536]{1,0:T(8,128)(2,1)S(1)} %copy-done.45), kind=kOutput, calls=%fused_computation.100 | convolution fusion | flops 7247757312 | bytes 20840448 | tf_op jit(solution)/shard_map/dot_general | solution.py:573
  237.2 30.1 %fusion.7 = (bf16[2048,1536]{1,0:T(8,128)(2,1)}, bf16[2048,1536]{1,0:T(8,128)(2,1)}, bf16[2048,1536]{1,0:T(8,128)(2,1)}) fusion(f32[2048,1536]{1,0:T(8,128)} %fusion.32, f32[2048,1536]{1,0:T(8,128)} %fusion.33, bf16[2048,1152]{1,0:T(8,128)(2,1)S(1)} %bitcast.84, bf16[1536,1152]{1,0:T(8,128)(2,1)} %get-tuple-element.35), kind=kOutput, calls=%fused_computation.10 | convolution fusion | flops 7320109056 | bytes 52297728 | tf_op jit(solution)/shard_map/dot_general | solution.py:573
  267.4 11.7 %convolution_convert_fusion.2.refs_2_ = bf16[1152,1536]{1,0:T(8,128)(2,1)} fusion(bf16[2048,1152]{1,0:T(8,128)(2,1)S(1)} %bitcast.80, bf16[2048,1536]{1,0:T(8,128)(2,1)} %get-tuple-element.47), kind=kOutput, calls=%fused_computation.15 | convolution fusion | flops 7249526784 | bytes 14548992 | tf_op jit(solution)/shard_map/dot_general | solution.py:573
  279.1 10.7 %fusion.34 = f32[2048,1152]{1,0:T(8,128)} fusion(bf16[2048,1536]{1,0:T(8,128)(2,1)S(1)} %copy-done.47, bf16[1152,1536]{1,0:T(8,128)(2,1)S(1)} %copy-done.46), kind=kOutput, calls=%fused_computation.102 | convolution fusion | flops 7247757312 | bytes 19267584 | tf_op jit(solution)/shard_map/dot_general | solution.py:573
  289.8 11.8 %add_convert_fusion = bf16[2048,1152]{1,0:T(8,128)(2,1)S(1)} fusion(f32[2048,1152]{1,0:T(8,128)} %fusion.34, bf16[2048,1536]{1,0:T(8,128)(2,1)} %get-tuple-element.47, bf16[1152,1536]{1,0:T(8,128)(2,1)S(1)} %copy-done.44), kind=kOutput, calls=%fused_computation.12 | convolution fusion | flops 7252475904 | bytes 23986176 | tf_op jit(solution)/shard_map/dot_general | solution.py:573
  302.1 3.6 copy-done.21
  305.7 12.2 %convolution_convert_fusion.1.refs_3_ = bf16[1536,1152]{1,0:T(8,128)(2,1)} fusion(bf16[2048,1536]{1,0:T(8,128)(2,1)} %get-tuple-element.49, bf16[2048,1152]{1,0:T(8,128)(2,1)S(1)} %bitcast.85), kind=kOutput, calls=%fused_computation.14 | convolution fusion | flops 7249526784 | bytes 14548992 | tf_op jit(solution)/shard_map/dot_general | solution.py:573
  317.9 10.4 %convolution_convert_fusion.4 = bf16[2048,1152]{1,0:T(8,128)(2,1)S(1)} fusion(bf16[2048,1536]{1,0:T(8,128)(2,1)} %get-tuple-element.49, bf16[1536,1152]{1,0:T(8,128)(2,1)S(1)} %copy-done.42), kind=kOutput, calls=%fused_computation.17 | convolution fusion | flops 7250116608 | bytes 14548992 | tf_op jit(solution)/shard_map/dot_general | solution.py:573
  330.0 4.5 fusion.29
  336.6 11.1 %convolution_convert_fusion.3.refs_1_ = bf16[1152,1536]{1,0:T(8,128)(2,1)} fusion(bf16[2048,1152]{1,0:T(8,128)(2,1)S(1)} %bitcast.83, bf16[2048,1536]{1,0:T(8,128)(2,1)} %get-tuple-element.48), kind=kOutput, calls=%fused_computation.16 | convolution fusion | flops 7249526784 | bytes 14548992 | tf_op jit(solution)/shard_map/dot_general | solution.py:573
  350.7 3.2 convolution_convert_fusion.6
  354.0 42.6 %attend_back.1 = (bf16[576,2048]{1,0:T(8,128)(2,1)}, bf16[384,2048]{1,0:T(8,128)(2,1)S(1)}) custom-call(s32[2]{0:T(128)S(1)} %bitcast.59, bf16[576,2048]{1,0:T(8,128)(2,1)} %copy-done.8, bf16[2048,384]{1,0:T(8,128)(2,1)S(1)} %copy-done.11, bf16[384,2048]{1,0:T(8,128)(2,1)} %copy-done.9, bf16[576,2048]{1,0:T(8,128)(2,1)} %get-tuple-element.36.ot_ref, ...), custom_call_target="tpu_custom_call" | custom-call | flops 33218887680 | bytes 28311552 | tf_op jit(solution)/shard_map/attend_back/pallas_call | solution.py:758
  400.2 6.5 %convolution_convert_fusion.5 = bf16[1152,960]{0,1:T(8,128)(2,1)} fusion(bf16[960,2048]{1,0:T(8,128)(2,1)S(1)} %constant_dynamic-update-slice_fusion, bf16[2048,1152]{1,0:T(8,128)(2,1)S(1)} %bitcast.91), kind=kOutput, calls=%fused_computation.40 | convolution fusion | flops 4530954240 | bytes 10862592 | tf_op jit(solution)/shard_map/dot_general | solution.py:573
  406.7 7.5 %convolution_convert_fusion = bf16[2048,1152]{1,0:T(8,128)(2,1)} fusion(bf16[960,2048]{1,0:T(8,128)(2,1)S(1)} %constant_dynamic-update-slice_fusion, bf16[1152,1536]{1,0:T(8,128)(2,1)S(1)} %copy-done.32), kind=kOutput, calls=%fused_computation.13 | convolution fusion | flops 4532207616 | bytes 11010048 | tf_op jit(solution)/shard_map/dot_general | solution.py:573
  417.0 3.4 constant_dynamic-slice_fusion.1
  421.2 9.5 %maximum_maximum_fusion.refs_0_ = bf16[1152,1536]{1,0:T(8,128)(2,1)} fusion(bf16[576,576]{1,0:T(8,128)(2,1)S(1)} %get-tuple-element.64, bf16[576,576]{1,0:T(8,128)(2,1)S(1)} %get-tuple-element.63, bf16[1152,960]{1,0:T(8,128)(2,1)S(1)} %copy.26), kind=kLoop, calls=%fused_computation.41 | loop fusion | flops 10616832 | bytes 7077888 | tf_op jit(solution)/shard_map/concatenate | solution.py:889
  430.7 164.8 %reduce_grads.1 = (bf16[144,3072]{1,0:T(8,128)(2,1)S(1)}, bf16[144,3072]{1,0:T(8,128)(2,1)S(1)}, bf16[144,3072]{1,0:T(8,128)(2,1)S(1)}, bf16[384,1152]{1,0:T(8,128)(2,1)S(1)}) custom-call(bf16[1152,1536]{1,0:T(8,128)(2,1)} %maximum_maximum_fusion.refs_0_, bf16[1152,1536]{1,0:T(8,128)(2,1)} %convolution_convert_fusion.3.refs_1_, ...), custom_call_target="tpu_custom_call" | custom-call | tf_op jit(solution)/shard_map/reduce_grads/pallas_call | solution.py:555
  598.4 3.5 fusion.30
  614.2 3.8 convert_multiply_fusion.4
  621.1 3.6 fusion.10
  624.8 8.6 %fusion.17 = (bf16[2,1,512,1152]{3,2,1,0:T(8,128)(2,1)}, bf16[2,1,512,1152]{3,2,1,0:T(8,128)(2,1)}) fusion(bf16[2,512,1152]{2,1,0:T(8,128)(2,1)} %collective-permute-done.8, f32[2,512]{1,0:T(2,128)S(1)} %broadcast_multiply_fusion.3, f32[2,512]{1,0:T(2,128)S(1)} %copy-done.37, bf16[2,1024,1152]{2,1,0:T(8,128)(2,1)} %bitcast.71, s32[]{:T(128)S(6)} %select_n.84, ...), kind=kLoop, calls=%fused_computation.44 | loop fusion | flops 28311552 | bytes 28327940 | tf_op jit(solution)/shard_map/reshape | solution.py:901
  (178 shorter events, 61.1 us)
Async XLA Ops:
  0.6 12.9 %copy-start.23 = (bf16[144,3072]{1,0:T(8,128)(2,1)S(1)}, bf16[144,3072]{1,0:T(8,128)(2,1)}, u32[]{:S(2)}) copy-start(bf16[144,3072]{1,0:T(8,128)(2,1)} %param.23) | copy-start | bytes 2654212
  0.7 12.9 %copy-start.25 = (bf16[144,3072]{1,0:T(8,128)(2,1)S(1)}, bf16[144,3072]{1,0:T(8,128)(2,1)}, u32[]{:S(2)}) copy-start(bf16[144,3072]{1,0:T(8,128)(2,1)} %param.22) | copy-start | bytes 2654212
  0.7 130.4 %collective-permute-start = (bf16[2,512,1152]{2,1,0:T(8,128)(2,1)}, bf16[2,512,1152]{2,1,0:T(8,128)(2,1)}, u32[]{:S(2)}, u32[]{:S(2)}) collective-permute-start(bf16[2,512,1152]{2,1,0:T(8,128)(2,1)} %bitcast.64), channel_id=1, source_target_pairs={{0,1},{1,0},{2,3},{3,2},{4,5},{5,4},{6,7},{7,6},{8,9},{9,8},{10,11... | collective-permute-start | bytes 7077896 | tf_op jit(solution)/shard_map/ppermute | solution.py:792
  3.6 11.6 %copy-start.40 = (f32[144]{0:T(256)}, f32[144]{0:T(256)S(1)}, u32[]{:S(2)}) copy-start(f32[144]{0:T(256)S(1)} %convert_element_type.145) | copy-start | bytes 1732
  126.8 2.4 collective-permute-start.1
  131.0 19.4 %copy-start = (bf16[576,1152]{1,0:T(8,128)(2,1)}, bf16[576,1152]{1,0:T(8,128)(2,1)S(1)}, u32[]{:S(2)}) copy-start(bf16[576,1152]{1,0:T(8,128)(2,1)S(1)} %pad_maximum_fusion.4.wo_ref) | copy-start | bytes 3981316
  136.2 14.2 %copy-start.2 = (s32[2,1]{0,1:T(1,128)S(1)}, s32[2,1]{0,1:T(1,128)}, u32[]{:S(2)}) copy-start(s32[2,1]{0,1:T(1,128)} %param.15) | copy-start | bytes 28
  150.4 40.9 %copy-start.9 = (bf16[384,2048]{1,0:T(8,128)(2,1)}, bf16[384,2048]{1,0:T(8,128)(2,1)S(1)}, u32[]{:S(2)}) copy-start(bf16[384,2048]{1,0:T(8,128)(2,1)S(1)} %get-tuple-element.31.vt_ref.kt_ref) | copy-start | bytes 4718596
  150.5 40.9 %copy-start.10 = (bf16[2048,384]{1,0:T(8,128)(2,1)}, bf16[2048,384]{1,0:T(8,128)(2,1)S(1)}, u32[]{:S(2)}) copy-start(bf16[2048,384]{1,0:T(8,128)(2,1)S(1)} %get-tuple-element.30.kv_ref) | copy-start | bytes 4718596
  194.6 4.9 collective-permute-start.2
  194.8 10.2 %collective-permute-start.5 = (bf16[2,512,1152]{2,1,0:T(8,128)(2,1)}, bf16[2,512,1152]{2,1,0:T(8,128)(2,1)}, u32[]{:S(2)}, u32[]{:S(2)}) collective-permute-start(bf16[2,512,1152]{2,1,0:T(8,128)(2,1)} %bitcast.9), channel_id=1, source_target_pairs={{0,1},{1,0},{2,3},{3,2},{4,5},{5,4},{6,7},{7,6},{8,9},{9,8},{10,11... | collective-permute-start | bytes 7077896 | tf_op jit(solution)/shard_map/ppermute | solution.py:792
  203.8 4.6 collective-permute-start.3
  211.8 55.5 %copy-start.19 = (bf16[2,1024,1152]{2,1,0:T(8,128)(2,1)}, bf16[2,1024,1152]{2,1,0:T(8,128)(2,1)S(1)}, u32[]{:S(2)}) copy-start(bf16[2,1024,1152]{2,1,0:T(8,128)(2,1)S(1)} %pad_maximum_fusion.1) | copy-start | bytes 14155780
  215.1 11.0 %copy-start.45 = (bf16[1152,1536]{1,0:T(8,128)(2,1)S(1)}, bf16[1152,1536]{1,0:T(8,128)(2,1)}, u32[]{:S(2)}) copy-start(bf16[1152,1536]{1,0:T(8,128)(2,1)} %get-tuple-element.33) | copy-start | bytes 10616836
  237.2 30.1 %copy-start.20 = (bf16[2,1024,1152]{2,1,0:T(8,128)(2,1)}, bf16[2,1024,1152]{2,1,0:T(8,128)(2,1)S(1)}, u32[]{:S(2)}) copy-start(bf16[2,1024,1152]{2,1,0:T(8,128)(2,1)S(1)} %pad_maximum_fusion.2) | copy-start | bytes 14155780
  267.3 11.8 %copy-start.46 = (bf16[1152,1536]{1,0:T(8,128)(2,1)S(1)}, bf16[1152,1536]{1,0:T(8,128)(2,1)}, u32[]{:S(2)}) copy-start(bf16[1152,1536]{1,0:T(8,128)(2,1)} %get-tuple-element.33) | copy-start | bytes 10616836
  267.3 11.7 %copy-start.47 = (bf16[2048,1536]{1,0:T(8,128)(2,1)S(1)}, bf16[2048,1536]{1,0:T(8,128)(2,1)}, u32[]{:S(2)}) copy-start(bf16[2048,1536]{1,0:T(8,128)(2,1)} %get-tuple-element.48) | copy-start | bytes 18874372
  279.1 10.7 %copy-start.44 = (bf16[1152,1536]{1,0:T(8,128)(2,1)S(1)}, bf16[1152,1536]{1,0:T(8,128)(2,1)}, u32[]{:S(2)}) copy-start(bf16[1152,1536]{1,0:T(8,128)(2,1)} %get-tuple-element.34) | copy-start | bytes 10616836
  301.7 27.8 %copy-start.17 = (bf16[2048,1152]{1,0:T(8,128)(2,1)}, bf16[2048,1152]{1,0:T(8,128)(2,1)S(1)}, u32[]{:S(2)}) copy-start(bf16[2048,1152]{1,0:T(8,128)(2,1)S(1)} %add_convert_fusion) | copy-start | bytes 14155780
  301.9 26.5 %collective-permute-start.6 = (bf16[2,512,1152]{2,1,0:T(8,128)(2,1)S(1)}, bf16[2,512,1152]{2,1,0:T(8,128)(2,1)S(1)}, u32[]{:S(2)}, u32[]{:S(2)}) collective-permute-start(bf16[2,512,1152]{2,1,0:T(8,128)(2,1)S(1)} %constant_dynamic-slice_fusion.2), channel_id=1, source_target_pairs={{0,1},{1,0},{2,3},{3,2},{4,5},{5,4},{6,7},{7,6},{8,9},{9,8},{10,11... | collective-permute-start | bytes 7077896 | tf_op jit(solution)/shard_map/ppermute | solution.py:792
  305.7 12.2 %copy-start.42 = (bf16[1536,1152]{1,0:T(8,128)(2,1)S(1)}, bf16[1536,1152]{1,0:T(8,128)(2,1)}, u32[]{:S(2)}) copy-start(bf16[1536,1152]{1,0:T(8,128)(2,1)} %get-tuple-element.35) | copy-start | bytes 10616836
  305.7 22.7 %slice-start = ((s8[4718592]{0:T(1024)(128)(4,1)}), s8[4194304]{0:T(1024)(128)(4,1)S(1)}, s32[]{:S(2)}) async-start(s8[4718592]{0:T(1024)(128)(4,1)} %bitcast.60), calls=%async_computation | async-start | bytes 8388608
  317.9 10.5 %slice-start.1 = ((s8[4718592]{0:T(1024)(128)(4,1)}), s8[524288]{0:T(1024)(128)(4,1)S(1)}, s32[]{:S(2)}) async-start(s8[4718592]{0:T(1024)(128)(4,1)} %bitcast.60), calls=%async_computation.1 | async-start | bytes 1048576
  317.9 10.5 %copy-start.36 = (f32[2,512]{1,0:T(2,128)S(1)}, f32[2,512]{1,0:T(2,128)}, u32[]{:S(2)}) copy-start(f32[2,512]{1,0:T(2,128)} %copy-done.35) | copy-start | bytes 12292
  334.4 13.3 %collective-permute-start.7 = (bf16[2,512,1152]{2,1,0:T(8,128)(2,1)S(1)}, bf16[2,512,1152]{2,1,0:T(8,128)(2,1)S(1)}, u32[]{:S(2)}, u32[]{:S(2)}) collective-permute-start(bf16[2,512,1152]{2,1,0:T(8,128)(2,1)S(1)} %fusion.29), channel_id=1, source_target_pairs={{0,1},{1,0},{2,3},{3,2},{4,5},{5,4},{6,7},{7,6},{8,9},{9,8},{10,11... | collective-permute-start | bytes 7077896 | tf_op jit(solution)/shard_map/ppermute | solution.py:792
  336.2 288.5 %collective-permute-start.4 = (bf16[2,512,1152]{2,1,0:T(8,128)(2,1)}, bf16[2,512,1152]{2,1,0:T(8,128)(2,1)}, u32[]{:S(2)}, u32[]{:S(2)}) collective-permute-start(bf16[2,512,1152]{2,1,0:T(8,128)(2,1)} %constant_dynamic-slice_fusion.3), channel_id=1, source_target_pairs={{0,1},{1,0},{2,3},{3,2},{4,5},{5,4},{6,7},{7,6},{8,9},{9,8},{10,11... | collective-permute-start | bytes 7077896 | tf_op jit(solution)/shard_map/ppermute | solution.py:792
  353.9 42.6 %copy-start.27 = (bf16[576,1152]{1,0:T(8,128)(2,1)}, bf16[576,1152]{1,0:T(8,128)(2,1)S(1)}, u32[]{:S(2)}) copy-start(bf16[576,1152]{1,0:T(8,128)(2,1)S(1)} %convolution_convert_fusion.6) | copy-start | bytes 3981316
  397.8 22.9 %collective-permute-start.9 = (bf16[576,576]{1,0:T(8,128)(2,1)}, bf16[576,576]{1,0:T(8,128)(2,1)S(1)}, u32[]{:S(2)}, u32[]{:S(2)}) collective-permute-start(bf16[576,576]{1,0:T(8,128)(2,1)} %constant_dynamic-slice_fusion), channel_id=1, source_target_pairs={{0,1},{1,0},{2,3},{3,2},{4,5},{5,4},{6,7},{7,6},{8,9},{9,8},{10,11... | collective-permute-start | bytes 1990664 | tf_op jit(solution)/shard_map/ppermute | solution.py:792
  420.4 200.8 %collective-permute-start.8 = (bf16[2,512,1152]{2,1,0:T(8,128)(2,1)}, bf16[2,512,1152]{2,1,0:T(8,128)(2,1)}, u32[]{:S(2)}, u32[]{:S(2)}) collective-permute-start(bf16[2,512,1152]{2,1,0:T(8,128)(2,1)} %constant_dynamic-slice_fusion.1), channel_id=1, source_target_pairs={{0,1},{1,0},{2,3},{3,2},{4,5},{5,4},{6,7},{7,6},{8,9},{9,8},{10,11... | collective-permute-start | bytes 7077896 | tf_op jit(solution)/shard_map/ppermute | solution.py:792
  598.4 15.8 %copy-start.24 = (bf16[144,3072]{1,0:T(8,128)(2,1)S(1)}, bf16[144,3072]{1,0:T(8,128)(2,1)}, u32[]{:S(2)}) copy-start(bf16[144,3072]{1,0:T(8,128)(2,1)} %param.23) | copy-start | bytes 2654212
  598.4 15.8 %copy-start.41 = (f32[144]{0:T(256)S(1)}, f32[144]{0:T(256)}, u32[]{:S(2)}) copy-start(f32[144]{0:T(256)} %copy-done.40) | copy-start | bytes 1732
  614.2 10.5 %slice-start.2 = ((s8[4718592]{0:T(1024)(128)(4,1)}), s8[4194304]{0:T(1024)(128)(4,1)S(1)}, s32[]{:S(2)}) async-start(s8[4718592]{0:T(1024)(128)(4,1)} %bitcast.62), calls=%async_computation.2 | async-start | bytes 8388608
  (35 other events, 170.6 us)
